TPU v7x, 256 devices: a whole 4x4x8 slice. The times are simulated.
256 devices in a mesh: blk: 64 (over z, x, core), grp: 4 (over y).
Axes of the slice: x: 4, y: 4, z: 8, core: 2. Of those that a mesh axis runs over, the one named last changes fastest.
Arguments:
- embeddings: bfloat16 [131072, 4096], P(('blk', 'grp')), may hold values from -40 to 40, as said below
- cluster_sizes: int32 [128], replicated, may hold values from 1 to 4096, 131072 in all
- sign_bits: int32 [4096], replicated, may hold values from 0 to 1
- sample_cols: int32 [1024], replicated, may hold values from 0 to 4095
Outputs:
- nearest: float32 [131072], P(('blk', 'grp'))
Inputs may be any that keep to these rules, and one draw needn't show every extreme that they name: embeddings: rows mix independent vectors with earlier rows at random weights. `cluster_sizes`: rows of each cluster in order; they sum to 131072, the largest is exactly 4096.
All inputs are finite; a program needn't handle non-finite values.
Results may differ from a plain program's by a relative error of at most 0.00043.
Values may be sent and summed in bfloat16 or wider, within the bound.
A program may use at most 64 MiB of HBM per device.

v0:
```python
import jax
import jax.numpy as jnp
from jax import lax
from jax.sharding import PartitionSpec as P

D = 4096
HB = 256
REACH = 2


def from_behind(shard, axis, by):
    count = lax.axis_size(axis)
    pairs = [(i, i + by) for i in range(count) if 0 <= i + by < count]
    return lax.ppermute(shard, axis, pairs)


def hadamard(order):
    indices = jnp.arange(order, dtype=jnp.int32)
    parity = jnp.zeros((order, order), jnp.int32)
    for place in range(order.bit_length() - 1):
        parity = parity + (indices[:, None] >> place & 1) * (indices[None, :] >> place & 1)
    return jnp.where(parity % 2 == 0, 1.0, -1.0).astype(jnp.bfloat16)


def sketch_rows(rows_emb, sign_bits, sample_cols):
    count = rows_emb.shape[0]
    flips = (2 * sign_bits - 1).astype(jnp.bfloat16)
    flipped = rows_emb * flips[None, :]
    table = hadamard(HB)
    mixed = jnp.einsum(
        "rbi,ij->rbj",
        flipped.reshape(count, D // HB, HB),
        table,
        preferred_element_type=jnp.float32,
    ).reshape(count, D)
    picked = jnp.take(mixed, sample_cols, axis=1)
    scale = lax.rsqrt(jnp.sum(picked * picked, axis=1, keepdims=True) + 1e-06)
    return (picked * scale).astype(jnp.bfloat16)


def cluster_of(first_row, count, ends):
    rows = first_row + jnp.arange(count, dtype=jnp.int32)
    return jnp.sum((ends[None, :] <= rows[:, None]).astype(jnp.int32), axis=1)


def local(embeddings, cluster_sizes, sign_bits, sample_cols):
    block = embeddings.shape[0]
    groups = lax.axis_size("grp")
    run_width = groups * block
    blk_pos = lax.axis_index("blk")
    blk_count = lax.axis_size("blk")
    sketch = sketch_rows(embeddings, sign_bits, sample_cols)
    ends = jnp.cumsum(cluster_sizes)
    group_first = blk_pos * run_width
    own_first = group_first + lax.axis_index("grp") * block
    own_ids = cluster_of(own_first, block, ends)
    own_rows = own_first + jnp.arange(block, dtype=jnp.int32)
    run_sketch = lax.all_gather(sketch, "grp", axis=0, tiled=True)

    def cosine_tile(remote, remote_first, allowed, self_pairs):
        remote_ids = cluster_of(remote_first, run_width, ends)
        paired = jnp.logical_and(own_ids[:, None] == remote_ids[None, :], allowed)
        if self_pairs:
            remote_rows = remote_first + jnp.arange(run_width, dtype=jnp.int32)
            paired = paired & (own_rows[:, None] != remote_rows[None, :])
        scores = lax.dot_general(
            sketch, remote, (((1,), (1,)), ((), ())), preferred_element_type=jnp.float32
        )
        masked = jnp.where(paired, scores, -1.0)
        return (jnp.max(masked, axis=1), jnp.max(masked, axis=0))

    nearest, unused_cols = cosine_tile(run_sketch, group_first, True, True)
    returned = jnp.full((run_width,), -1.0, jnp.float32)
    for reach in range(1, REACH + 1):
        lower_run = from_behind(run_sketch, "blk", reach)
        rows_best, cols_best = cosine_tile(
            lower_run, group_first - reach * run_width, blk_pos >= reach, False
        )
        nearest = jnp.maximum(nearest, rows_best)
        arrived = from_behind(cols_best, "blk", -reach)
        returned = jnp.where(blk_pos + reach < blk_count, jnp.maximum(returned, arrived), returned)
    merged = lax.pmax(returned, "grp")
    own_share = lax.dynamic_slice_in_dim(merged, lax.axis_index("grp") * block, block)
    nearest = jnp.maximum(nearest, own_share)
    return nearest


def solution(mesh):
    placed = (P(("blk", "grp"), None), P(), P(), P())
    return jax.shard_map(
        local, mesh=mesh, in_specs=placed, out_specs=P(("blk", "grp")), check_vma=False
    )
```

profile of v0, /device:TPU:128, one launch (start us, length us, event | category | flops | bytes accessed | tf_op | source)
XLA Modules:
  0.0 251.0 jit_solution(12665161408694175027)
XLA Ops:
  6.5 0.0 all-gather.2.cloned.1.call-start
  6.6 0.7 fusion.32
  7.3 0.7 compare_and_fusion
  7.9 0.7 add_convert_fusion
  8.7 2.5 broadcast_multiply_fusion
  11.1 5.2 %fusion = f32[512,16,256]{0,2,1:T(8,128)} fusion(bf16[64,16,8,256]{3,2,1,0:T(8,128)(2,1)S(1)} %bitcast.18, s32[256]{0:T(256)S(1)} %get-tuple-element.14, s32[256]{0:T(256)S(1)} %get-tuple-element.15, s32[256]{0:T(256)S(1)} %get-tuple-element.16, s32[256]{0:T(256)S(1)} %get-tuple-element.17, s32[256]{0:T(256)S(1)} %get-tuple-element.18, ...), kind=kOutput, calls=%fused_computation.1 | convolution fusion | flops 1075642368 | bytes 12591104 | tf_op jit(solution)/shard_map/rbi,ij->rbj/dot_general | solution.py:30
  16.3 7.4 %gather_fusion = f32[1024,512]{1,0:T(8,128)S(1)} fusion(f32[512,4096]{0,1:T(8,128)} %bitcast.17, s32[1024]{0:T(1024)S(1)} %fusion.32), kind=kCustom, calls=%fused_computation | custom fusion | bytes 4198400 | tf_op jit(solution)/shard_map/jit(_take)/gather | solution.py:36
  23.7 0.0 copy-start
  23.7 0.3 multiply_reduce_fusion
  24.0 1.2 fusion.45
  25.3 0.0 all-gather.2.cloned.1.call-update
  25.3 52.5 %all-gather.2.cloned.1.call-done = bf16[2048,1024]{0,1:T(8,128)(2,1)} async-done(((bf16[512,1024]{0,1:T(8,128)(2,1)}), bf16[2048,1024]{0,1:T(8,128)(2,1)}) %all-gather.2.cloned.1.call-update) | async-done | bytes 4194320 | tf_op jit(solution)/shard_map/all_gather | solution.py:58
  77.8 3.4 %collective-permute-start.1 = (bf16[2048,1024]{0,1:T(8,128)(2,1)}, bf16[2048,1024]{0,1:T(8,128)(2,1)}, u32[]{:S(2)}, u32[]{:S(2)}) collective-permute-start(bf16[2048,1024]{0,1:T(8,128)(2,1)} %all-gather.2.cloned.1.call-done), channel_id=1, source_target_pairs={{0,8},{4,12},{8,16},{12,20},{16,24},{20,28},{24,32},{28,36},{32,40... | collective-permute-start | bytes 12582920 | tf_op jit(solution)/shard_map/ppermute | solution.py:14
  81.2 1.9 collective-permute-start
  83.1 0.0 copy-done
  83.1 0.1 copy.9
  83.3 0.2 reduce-window.8
  83.4 0.1 reduce.1
  83.6 0.2 convert_reduce_fusion.3
  83.8 2.4 convert_reduce_fusion.2
  86.2 0.3 multiply_convert_fusion
  86.4 90.4 %collective-permute-done.1 = bf16[2048,1024]{0,1:T(8,128)(2,1)} collective-permute-done((bf16[2048,1024]{0,1:T(8,128)(2,1)}, bf16[2048,1024]{0,1:T(8,128)(2,1)}, u32[]{:S(2)}, u32[]{:S(2)}) %collective-permute-start.1) | collective-permute-done | bytes 4194336 | tf_op jit(solution)/shard_map/ppermute | solution.py:14
  176.8 4.6 %fusion.38 = f32[512,2048]{1,0:T(8,128)S(1)} fusion(bf16[1024,512]{1,0:T(8,128)(2,1)S(1)} %multiply_convert_fusion, bf16[2048,1024]{0,1:T(8,128)(2,1)} %collective-permute-done.1), kind=kOutput, calls=%fused_computation.70 | convolution fusion | flops 2147483648 | bytes 9437184 | tf_op jit(solution)/shard_map/dot_general | solution.py:66
  181.4 39.2 %collective-permute-done = bf16[2048,1024]{0,1:T(8,128)(2,1)} collective-permute-done((bf16[2048,1024]{0,1:T(8,128)(2,1)}, bf16[2048,1024]{0,1:T(8,128)(2,1)}, u32[]{:S(2)}, u32[]{:S(2)}) %collective-permute-start) | collective-permute-done | bytes 4194336 | tf_op jit(solution)/shard_map/ppermute | solution.py:14
  220.6 0.0 copy-start.1
  220.6 6.5 %fusion.4 = (f32[512]{0:T(512)S(1)}, f32[2048]{0:T(1024)S(1)}, f32[2048]{0:T(1024)S(1)}, f32[512]{0:T(512)S(1)}) fusion(s32[2048]{0:T(1024)S(1)} %get-tuple-element.12, s32[512]{0:T(512)S(1)} %convert_reduce_fusion.3, pred[]{:T(512)S(6)} %ge.14, f32[512,2048]{1,0:T(8,128)S(1)} %fusion.38, pred[]{:T(512)S(6)} %ge.15, s32[2048]{0:T(1024)S(1)} %get-tuple-element.13, ...), kind=kOutput, calls=%fused_computation.8 | convolution fusion | flops 2157964288 | bytes 9476098 | tf_op jit(solution)/shard_map/dot_general | solution.py:66
  227.1 1.9 collective-permute-start.2
  229.0 1.9 collective-permute-start.3
  230.9 0.0 copy-done.1
  230.9 2.9 %select_reduce_fusion = f32[512]{0:T(512)S(1)} fusion(bf16[1024,512]{1,0:T(8,128)(2,1)S(1)} %multiply_convert_fusion, bf16[2048,1024]{0,1:T(8,128)(2,1)S(1)} %copy-done.1, s32[2048]{0:T(1024)S(1)} %iota_add_fusion.2, s32[2048]{0:T(1024)S(1)} %get-tuple-element.11, s32[512]{0:T(512)S(1)} %iota_add_fusion.3, s32[512]{0:T(512)S(1)} %convert_reduce_fusion.3), kind=kOutput, calls=%fused_computation.4 | convolution fusion | flops 2152726016 | bytes 5265408 | tf_op jit(solution)/shard_map/dot_general | solution.py:66
  233.8 0.0 collective-permute-done.2
  233.8 0.7 collective-permute-done.3
  234.5 9.0 %pmax.7 = f32[2048]{0:T(1024)S(1)} all-reduce(f32[2048]{0:T(1024)S(1)} %maximum_select_fusion), channel_id=1, replica_groups=mesh['blk'=64,'grp'=4] {'grp'}, use_global_device_ids=true, to_apply=%region_11.12 | all-reduce | flops 2048 | bytes 16384 | tf_op jit(solution)/shard_map/pmax | solution.py:82
  243.5 0.7 dynamic-slice_maximum_fusion
  (9 shorter events, 0.0 us)
Async XLA Ops:
  6.5 71.3 %all-gather.2.cloned.1.call-start = ((), (), s32[]{:S(2)}) async-start(), calls=%async_computation | async-start | bytes 5242880 | tf_op jit(solution)/shard_map/all_gather | solution.py:58
  23.7 59.4 %copy-start = (s32[128]{0:T(128)S(1)}, s32[128]{0:T(128)}, u32[]{:S(2)}) copy-start(s32[128]{0:T(128)} %param.5) | copy-start | bytes 1540
  77.8 99.0 %collective-permute-start.1 = (bf16[2048,1024]{0,1:T(8,128)(2,1)}, bf16[2048,1024]{0,1:T(8,128)(2,1)}, u32[]{:S(2)}, u32[]{:S(2)}) collective-permute-start(bf16[2048,1024]{0,1:T(8,128)(2,1)} %all-gather.2.cloned.1.call-done), channel_id=1, source_target_pairs={{0,8},{4,12},{8,16},{12,20},{16,24},{20,28},{24,32},{28,36},{32,40... | collective-permute-start | bytes 12582920 | tf_op jit(solution)/shard_map/ppermute | solution.py:14
  81.2 139.4 %collective-permute-start = (bf16[2048,1024]{0,1:T(8,128)(2,1)}, bf16[2048,1024]{0,1:T(8,128)(2,1)}, u32[]{:S(2)}, u32[]{:S(2)}) collective-permute-start(bf16[2048,1024]{0,1:T(8,128)(2,1)} %all-gather.2.cloned.1.call-done), channel_id=1, source_target_pairs={{0,4},{4,8},{8,12},{12,16},{16,20},{20,24},{24,28},{28,32},{32,36}... | collective-permute-start | bytes 12582920 | tf_op jit(solution)/shard_map/ppermute | solution.py:14
  220.6 10.4 %copy-start.1 = (bf16[2048,1024]{0,1:T(8,128)(2,1)S(1)}, bf16[2048,1024]{0,1:T(8,128)(2,1)}, u32[]{:S(2)}) copy-start(bf16[2048,1024]{0,1:T(8,128)(2,1)} %all-gather.2.cloned.1.call-done) | copy-start | bytes 12582916
  227.1 6.8 %collective-permute-start.2 = (f32[2048]{0:T(1024)S(1)}, f32[2048]{0:T(1024)S(1)}, u32[]{:S(2)}, u32[]{:S(2)}) collective-permute-start(f32[2048]{0:T(1024)S(1)} %get-tuple-element.6), channel_id=1, source_target_pairs={{4,0},{8,4},{12,8},{16,12},{20,16},{24,20},{28,24},{32,28},{36,32}... | collective-permute-start | bytes 24584 | tf_op jit(solution)/shard_map/ppermute | solution.py:14
  229.0 5.5 %collective-permute-start.3 = (f32[2048]{0:T(1024)S(1)}, f32[2048]{0:T(1024)S(1)}, u32[]{:S(2)}, u32[]{:S(2)}) collective-permute-start(f32[2048]{0:T(1024)S(1)} %get-tuple-element.9), channel_id=1, source_target_pairs={{8,0},{12,4},{16,8},{20,12},{24,16},{28,20},{32,24},{36,28},{40,32... | collective-permute-start | bytes 24584 | tf_op jit(solution)/shard_map/ppermute | solution.py:14
Sparse Core Ops, SparseCore 0:
  25.4 52.3 all-gather.1
where the time goes:
time: 252 us; the launch traced here: 251 us
  waiting for transfers between devices  183 us (73%)
  matrix products  19.1 us (8%)
  between operations  13.6 us (5%)
  other arithmetic  9.94 us (4%)
  starting transfers between devices  9.13 us (4%)
  blocking collectives  8.97 us (4%)
  local copies, waits for them, and re-layouts  7.52 us (3%)
    ppermute x4, waiting for transfers between devices, from_behind(): return lax.ppermute(shard, axis, pairs)  130 us
    all_gather x1, waiting for transfers between devices, local(): run_sketch = lax.all_gather(sketch, 'grp', axis=0, tiled=True)  52.5 us
    dot_general x3, matrix products, cosine_tile(): lax.dot_general(sketch, remote, (((1,), (1,)), ((), ())), preferred_eleme...  14 us
    ppermute x4, starting transfers between devices, from_behind(): return lax.ppermute(shard, axis, pairs)  9.13 us
    pmax x1, blocking collectives, local(): merged = lax.pmax(returned, 'grp')  8.97 us
    gather x1, local copies, waits for them, and re-layouts, sketch_rows(): picked = jnp.take(mixed, sample_cols, axis=1)  7.4 us
    dot_general x1, matrix products, sketch_rows(): jnp.einsum('rbi,ij->rbj', flipped.reshape(count, D // HB, HB), table, pre...  5.16 us
  transfers between devices with their start and end apart: 5, of which 4 were waited for; matrix products, arithmetic and copies ran while one was open for 4% of the time, Pallas kernels for 0%

commit v1 on v0

v1 whole, which is shorter than its diff:
```python
import functools

import jax
import jax.numpy as jnp
from jax import lax
from jax.experimental import pallas as pl
from jax.experimental.pallas import tpu as pltpu
from jax.sharding import PartitionSpec as P

HB = 256
MESH = pl.DeviceIdType.MESH
F32 = jnp.float32
BF16 = jnp.bfloat16

A0, A1, A2, X0, B0, Y0, Z, W = range(8)
KINDS = 8


def parity_sign(bits):
    bits = bits ^ (bits >> 2)
    bits = bits ^ (bits >> 1)
    return (1 - 2 * (bits & 1)).astype(F32)


def kernel(blocks, groups, chunks, emb_ref, sizes_ref, sign_ref, cols_ref, out_ref, held, x_in, table, picked, row_best,
           lane_best, row_id, lane_id, landed, load_sem, send_sem, recv_sem, back_send, back_recv):
    rows, width = x_in.shape
    kept = table.shape[1]
    part = rows // chunks
    columns = blocks // 2
    blk = lax.axis_index("blk")
    y = lax.axis_index("grp")
    core = lax.rem(blk, 2)
    t = blk // 2
    step = 2 * core - 1

    def wrap(v, n):
        return lax.rem(v + 2 * n, n)

    y_on, y_back, y_two = wrap(y + step, groups), wrap(y - step, groups), wrap(y + 2, groups)
    t_on, t_back = wrap(t + step, columns), wrap(t - step, columns)
    own_on, own_back = 2 * t_on + core, 2 * t_back + core
    other, other_on = 2 * t + 1 - core, 2 * t_on + 1 - core
    z_to = 2 * wrap(t + core, columns) + 1 - core
    z_from = 2 * wrap(t - 1 + core, columns) + 1 - core

    partners = [
        (blk, y_on), (blk, y_back), (blk, y_two), (own_on, y), (own_back, y), (other, y), (other_on, y),
        (z_to, y_on), (z_from, y_back),
    ]
    barrier = pltpu.get_barrier_semaphore()
    for device in partners:
        pl.semaphore_signal(barrier, inc=1, device_id=device, device_id_type=MESH)

    loads = [
        pltpu.make_async_copy(emb_ref.at[pl.ds(c * part, part)], x_in.at[pl.ds(c * part, part)], load_sem.at[c])
        for c in range(chunks)
    ]
    for load in loads:
        load.start()

    cols = cols_ref[...]
    nibble = lax.broadcasted_iota(jnp.int32, (16, kept), 0)
    low = parity_sign(nibble & (cols & 15)).astype(F32)
    high = parity_sign(nibble & ((cols >> 4) & 15)).astype(F32)
    for u in range(16):
        picked[pl.ds(u * 16, 16), :] = low * high[u:u + 1, :]

    def fill(run, carry):
        chosen = jnp.where((cols >> 8) == run, 1.0, 0.0)
        table[pl.ds(pl.multiple_of(run * HB, HB), HB), :] = (picked[pl.ds(0, HB), :] * chosen).astype(BF16)
        return carry

    lax.fori_loop(0, width // HB, fill, 0)

    n_clusters = sizes_ref.shape[1]
    at = lax.broadcasted_iota(jnp.int32, (n_clusters, n_clusters), 0)
    upto = lax.broadcasted_iota(jnp.int32, (n_clusters, n_clusters), 1)
    ends = jnp.sum(jnp.where(upto <= at, sizes_ref[...], 0), axis=1, keepdims=True)

    def number(column, of_core, place):
        return (2 * column + of_core) * groups + place

    numbers = [
        number(t, core, y), number(t, core, y_back), number(t, core, y_two), number(t_back, core, y),
        number(t, 1 - core, y), number(t_on, 1 - core, y), number(wrap(t + core, columns), 1 - core, y_on),
        number(wrap(t - 1, columns), 1, groups - 1),
    ]
    for slot, block in enumerate(numbers):
        which = block * rows + lax.broadcasted_iota(jnp.int32, (n_clusters, rows), 1)
        ids = jnp.sum(jnp.where(ends <= which, 1.0, 0.0), axis=0, keepdims=True)
        lane_id[pl.ds(slot * 8, 8), :] = jnp.broadcast_to(ids, (8, rows))
        if slot in (A0, A1, A2, B0):
            row_id[pl.ds(slot * rows, rows), :] = jnp.broadcast_to(ids, (128, rows)).T
    row_best[...] = jnp.full_like(row_best, -1.0)
    lane_best[...] = jnp.full_like(lane_best, -1.0)

    def copy(source, target, c, device):
        return pltpu.make_async_remote_copy(
            src_ref=held.at[pl.ds(source * rows + c * part, part)],
            dst_ref=held.at[pl.ds(target * rows + c * part, part)],
            send_sem=send_sem.at[target, c],
            recv_sem=recv_sem.at[target, c],
            device_id=device,
            device_id_type=MESH,
        )

    def tile(left, left_at, count, right, right_at, lanes, own):
        rows_at = left * rows + left_at
        if not isinstance(rows_at, int):
            rows_at = pl.multiple_of(rows_at, 128)
        other_at = right * rows + right_at
        if not isinstance(other_at, int):
            other_at = pl.multiple_of(other_at, 128)
        scores = lax.dot_general(
            held[pl.ds(rows_at, count), :], held[pl.ds(other_at, lanes), :], (((1,), (1,)), ((), ())),
            preferred_element_type=F32,
        )
        left_ids = row_id[pl.ds(rows_at, count), :]
        best = row_best[pl.ds(rows_at, count), :]
        lane_row = right * 8 if isinstance(right, int) else pl.multiple_of(right * 8, 8)
        for j in range(lanes // 128):
            span = pl.ds(right_at + j * 128, 128)
            paired = left_ids == lane_id[pl.ds(lane_row, 8), span][0:1, :]
            if own:
                mine = left_at + lax.broadcasted_iota(jnp.int32, (count, 128), 0)
                theirs = right_at + j * 128 + lax.broadcasted_iota(jnp.int32, (count, 128), 1)
                paired = paired & (mine != theirs)
            masked = jnp.where(paired, scores[:, j * 128:(j + 1) * 128], -1.0)
            best = jnp.maximum(best, masked)
            if not own:
                lane_best[pl.ds(lane_row, 8), span] = jnp.maximum(
                    lane_best[pl.ds(lane_row, 8), span], jnp.max(masked.reshape(count // 8, 8, 128), axis=0)
                )
        row_best[pl.ds(rows_at, count), :] = best

    def tiles(left, right, left_part=None, right_part=None, own=False):
        for lc in range(chunks) if left_part is None else (left_part,):
            for rc in range(chunks) if right_part is None else (right_part,):
                tile(left, lc * part, part, right, rc * part, part, own)

    def close(slot):
        turned = row_best[pl.ds(slot * rows, rows), :].T
        lane_best[pl.ds(slot * 8, 8), :] = jnp.maximum(
            lane_best[pl.ds(slot * 8, 8), :], jnp.max(turned.reshape(16, 8, rows), axis=0)
        )

    signs = (2 * sign_ref[...] - 1).astype(F32).astype(BF16)
    sent = []
    for c in range(chunks):
        loads[c].wait()
        here = pl.ds(c * part, part)
        x_in[here, :] = x_in[here, :] * signs

        def project(n, total):
            span = pl.ds(pl.multiple_of(n * 256, 256), 256)
            some = jnp.dot(x_in[here, :], table[:, span], preferred_element_type=F32)
            picked[:, span] = some
            return total + some[:, :128] * some[:, :128] + some[:, 128:] * some[:, 128:]

        total = lax.fori_loop(0, kept // 256, project, jnp.zeros((part, 128), F32))
        scale = lax.rsqrt(jnp.sum(total, axis=1, keepdims=True) + 1e-6)
        held[here, :] = (picked[...] * scale).astype(BF16)
        if c == 0:
            pl.semaphore_wait(barrier, len(partners))
        for target, device in ((A1, (blk, y_on)), (X0, (own_on, y)), (B0, (other, y))):
            out = copy(A0, target, c, device)
            out.start()
            sent.append(out)

    tiles(A0, A0, own=True)
    for c in range(chunks):
        copy(A0, B0, c, (other, y)).wait_recv()

    @pl.when(core == 1)
    def _():
        tiles(A0, B0)

    z_core0 = [copy(A1, Z, c, (other_on, y)) for c in range(chunks)]
    z_core1 = [copy(A1, Z, c, (other, y)) for c in range(chunks)]
    w_out = [copy(A1, W, c, (other_on, y)) for c in range(chunks)]
    for c in range(chunks):
        copy(A0, A1, c, (blk, y_on)).wait_recv()
        out = copy(A1, A2, c, (blk, y_on))
        out.start()
        sent.append(out)

        @pl.when(core == 0)
        def _():
            z_core0[c].start()

        @pl.when(core == 1)
        def _():
            z_core1[c].start()

        @pl.when(jnp.logical_and(core == 1, y == 0))
        def _():
            w_out[c].start()

        copy(A0, X0, c, (own_on, y)).wait_recv()
        out = copy(X0, Y0, c, (other, y))
        out.start()
        sent.append(out)
        tiles(A1, A0, left_part=c)
        tiles(A0, X0, right_part=c)
    tiles(A1, X0)
    for c in range(chunks):
        copy(X0, Y0, c, (other, y)).wait_recv()

    @pl.when(core == 0)
    def _():
        tiles(A1, B0)
        tiles(A0, Y0)

    @pl.when(core == 1)
    def _():
        tiles(A1, Y0)

    for c in range(chunks):
        copy(A1, A2, c, (blk, y_on)).wait_recv()
        tiles(A2, A0, left_part=c)
        tiles(A2, X0, left_part=c)

        @pl.when(core == 0)
        def _():
            tiles(A2, Y0, left_part=c)

        @pl.when(core == 1)
        def _():
            tiles(A2, B0, left_part=c)

        copy(A1, Z, c, (other, y)).wait_recv()
        tiles(A2, Z, left_part=c, right_part=c)
        for before in range(c):
            tiles(A2, Z, left_part=c, right_part=before)
            tiles(A2, Z, left_part=before, right_part=c)

    @pl.when(jnp.logical_and(core == 1, y == groups - 1))
    def _():
        tiles(B0, Z)
        close(B0)

    @pl.when(jnp.logical_and(core == 0, y == 0))
    def _():
        for c in range(chunks):
            copy(A1, W, c, (other, y)).wait_recv()
        tiles(B0, W)
        close(B0)

    for slot in (A0, A1, A2):
        close(slot)

    def give(slot, device):
        return pltpu.make_async_remote_copy(
            src_ref=lane_best.at[pl.ds(slot * 8, 8)],
            dst_ref=landed.at[pl.ds(slot * 8, 8)],
            send_sem=back_send.at[slot],
            recv_sem=back_recv.at[slot],
            device_id=device,
            device_id_type=MESH,
        )

    back = [
        give(A1, (blk, y_back)), give(A2, (blk, y_two)), give(X0, (own_back, y)), give(B0, (other, y)),
        give(Y0, (other_on, y)), give(Z, (z_to, y_on)),
    ]
    w_back = give(W, (2 * wrap(t - 1, columns) + 1, groups - 1))
    for out in back:
        out.start()

    @pl.when(jnp.logical_and(core == 0, y == 0))
    def _():
        w_back.start()

    best = lane_best[pl.ds(A0 * 8, 8), :]
    for out, slot in zip(back, (A1, A2, X0, B0, Y0, Z), strict=True):
        out.wait_recv()
        best = jnp.maximum(best, landed[pl.ds(slot * 8, 8), :])
    out_ref[...] = jnp.max(best, axis=0, keepdims=True)

    @pl.when(jnp.logical_and(core == 1, y == groups - 1))
    def _():
        w_back.wait_recv()
        out_ref[...] = jnp.maximum(out_ref[...], jnp.max(landed[pl.ds(W * 8, 8), :], axis=0, keepdims=True))

    for out in (*sent, *back):
        out.wait_send()
    for c in range(chunks):
        z_core0[c].wait_send()

        @pl.when(jnp.logical_and(core == 1, y == 0))
        def _():
            w_out[c].wait_send()

    @pl.when(jnp.logical_and(core == 0, y == 0))
    def _():
        w_back.wait_send()


def solution(mesh):
    blocks, groups = mesh.shape["blk"], mesh.shape["grp"]
    chunks = 2

    def local(embeddings, cluster_sizes, sign_bits, sample_cols):
        rows, width = embeddings.shape
        kept = sample_cols.shape[0]
        vmem = pl.BlockSpec(memory_space=pltpu.VMEM)
        best = pl.pallas_call(
            functools.partial(kernel, blocks, groups, chunks),
            out_shape=jax.ShapeDtypeStruct((1, rows), F32),
            in_specs=[pl.BlockSpec(memory_space=pl.ANY), vmem, vmem, vmem],
            out_specs=vmem,
            scratch_shapes=[
                pltpu.VMEM((8 * rows, kept), BF16),
                pltpu.VMEM((rows, width), BF16),
                pltpu.VMEM((width, kept), BF16),
                pltpu.VMEM((rows // chunks, kept), F32),
                pltpu.VMEM((5 * rows, 128), F32),
                pltpu.VMEM((64, rows), F32),
                pltpu.VMEM((5 * rows, 128), F32),
                pltpu.VMEM((64, rows), F32),
                pltpu.VMEM((64, rows), F32),
                pltpu.SemaphoreType.DMA((chunks,)),
                pltpu.SemaphoreType.DMA((KINDS, chunks)),
                pltpu.SemaphoreType.DMA((KINDS, chunks)),
                pltpu.SemaphoreType.DMA((KINDS,)),
                pltpu.SemaphoreType.DMA((KINDS,)),
            ],
            compiler_params=pltpu.CompilerParams(
                collective_id=0, has_side_effects=True, vmem_limit_bytes=48 * 1024 * 1024
            ),
        )(embeddings, cluster_sizes.reshape(1, -1), sign_bits.reshape(1, -1), sample_cols.reshape(1, -1))
        return best.reshape(rows)

    placed = (P(("blk", "grp"), None), P(), P(), P())
    return jax.shard_map(local, mesh=mesh, in_specs=placed, out_specs=P(("blk", "grp")), check_vma=False)
```

time: 252 us -> 48.2 us (0.19)
  the two profiles are of different devices: /device:TPU:128 before, /device:TPU:8 now
where the time goes in v1:
time: 48.2 us; the launch traced here: 48 us
  Pallas kernels  43.1 us (89%)
  local copies, waits for them, and re-layouts  4.83 us (10%)
    pallas_call x1, Pallas kernels, local(): pl.pallas_call(functools.partial(kernel, blocks, groups, chunks), out_sha...  43.1 us
    unnamed x9, local copies, waits for them, and re-layouts  4.83 us

profile of v1, /device:TPU:8, one launch (start us, length us, event | category | flops | bytes accessed | tf_op | source)
XLA Modules:
  0.0 48.0 jit_solution(17052471343879341093)
XLA Ops:
  0.0 0.0 copy-start
  0.0 2.2 %copy-done = bf16[512,4096]{1,0:T(8,128)(2,1)S(1)} copy-done((bf16[512,4096]{1,0:T(8,128)(2,1)S(1)}, bf16[512,4096]{1,0:T(8,128)(2,1)}, u32[]{:S(2)}) %copy-start) | copy-done | bytes 4194328
  2.2 0.0 copy-start.1
  2.2 0.7 %copy-done.1 = s32[4096]{0:T(1024)S(1)} copy-done((s32[4096]{0:T(1024)S(1)}, s32[4096]{0:T(1024)}, u32[]{:S(2)}) %copy-start.1) | copy-done | bytes 16408
  2.9 0.0 copy-start.2
  2.9 0.7 %copy-done.2 = s32[1024]{0:T(1024)S(1)} copy-done((s32[1024]{0:T(1024)S(1)}, s32[1024]{0:T(1024)}, u32[]{:S(2)}) %copy-start.2) | copy-done | bytes 4120
  3.6 0.0 copy-start.3
  3.6 0.7 %copy-done.3 = s32[128]{0:T(128)S(1)} copy-done((s32[128]{0:T(128)S(1)}, s32[128]{0:T(128)}, u32[]{:S(2)}) %copy-start.3) | copy-done | bytes 536
  4.2 43.1 %shard_map.46 = f32[1,512]{1,0:T(1,128)S(1)} custom-call(bf16[512,4096]{1,0:T(8,128)(2,1)S(1)} %copy-done, s32[1,128]{1,0:T(1,128)S(1)} %bitcast.7, s32[1,4096]{1,0:T(1,128)S(1)} %bitcast.4, s32[1,1024]{1,0:T(1,128)S(1)} %bitcast.6), custom_call_target="tpu_custom_call" | custom-call | tf_op jit(solution)/shard_map/pallas_call | solution.py:308
  47.4 0.6 %copy.6 = f32[512]{0:T(512)} copy(f32[512]{0:T(512)S(1)} %bitcast.5) | data formatting | bytes 4096
Async XLA Ops:
  0.0 2.2 %copy-start = (bf16[512,4096]{1,0:T(8,128)(2,1)S(1)}, bf16[512,4096]{1,0:T(8,128)(2,1)}, u32[]{:S(2)}) copy-start(bf16[512,4096]{1,0:T(8,128)(2,1)} %emb_ref.1) | copy-start | bytes 12582916
  2.2 0.7 %copy-start.1 = (s32[4096]{0:T(1024)S(1)}, s32[4096]{0:T(1024)}, u32[]{:S(2)}) copy-start(s32[4096]{0:T(1024)} %param.6) | copy-start | bytes 49156
  2.9 0.7 %copy-start.2 = (s32[1024]{0:T(1024)S(1)}, s32[1024]{0:T(1024)}, u32[]{:S(2)}) copy-start(s32[1024]{0:T(1024)} %param.7) | copy-start | bytes 12292
  3.6 0.7 %copy-start.3 = (s32[128]{0:T(128)S(1)}, s32[128]{0:T(128)}, u32[]{:S(2)}) copy-start(s32[128]{0:T(128)} %param.5) | copy-start | bytes 1540

commit v2 on v1

v2 whole, which is shorter than its diff:
```python
import functools

import jax
import jax.numpy as jnp
from jax import lax
from jax.experimental import pallas as pl
from jax.experimental.pallas import tpu as pltpu
from jax.sharding import PartitionSpec as P

HB = 256
MESH = pl.DeviceIdType.MESH
F32 = jnp.float32
BF16 = jnp.bfloat16

A0, A1, A2, X0, B0, Y0, Z, W = range(8)
KINDS = 8


def parity_sign(bits):
    bits = bits ^ (bits >> 2)
    bits = bits ^ (bits >> 1)
    return (1 - 2 * (bits & 1)).astype(F32)


def kernel(blocks, groups, chunks, emb_ref, sizes_in, sign_in, cols_in, out_ref, sizes_ref, sign_ref, cols_ref, held, x_in,
           table, picked, row_best, lane_best, row_id, lane_id, landed, load_sem, small_sem, send_sem, recv_sem, back_send,
           back_recv):
    rows, width = x_in.shape
    kept = table.shape[1]
    part = rows // chunks
    columns = blocks // 2
    blk = lax.axis_index("blk")
    y = lax.axis_index("grp")
    core = lax.rem(blk, 2)
    t = blk // 2
    step = 2 * core - 1

    def wrap(v, n):
        return lax.rem(v + 2 * n, n)

    y_on, y_back, y_two = wrap(y + step, groups), wrap(y - step, groups), wrap(y + 2, groups)
    t_on, t_back = wrap(t + step, columns), wrap(t - step, columns)
    own_on, own_back = 2 * t_on + core, 2 * t_back + core
    other, other_on = 2 * t + 1 - core, 2 * t_on + 1 - core
    z_to = 2 * wrap(t + core, columns) + 1 - core

    has_on = jnp.logical_and(t + step >= 0, t + step < columns)
    has_back = jnp.logical_and(t - step >= 0, t - step < columns)
    has_z = jnp.logical_or(core == 0, t < columns - 1)

    barrier = pltpu.get_barrier_semaphore()

    def greet(*devices):
        for device in devices:
            pl.semaphore_signal(barrier, inc=1, device_id=device, device_id_type=MESH)

    small = [
        pltpu.make_async_copy(source, target, small_sem.at[i])
        for i, (source, target) in enumerate(((cols_in, cols_ref), (sizes_in, sizes_ref), (sign_in, sign_ref)))
    ]
    for load in small:
        load.start()

    greet((blk, y_on), (blk, y_back), (blk, y_two), (other, y))

    @pl.when(core == 0)
    def _():
        greet((other, y_on))

    @pl.when(core == 1)
    def _():
        greet((other, y_back))

    @pl.when(has_on)
    def _():
        greet((own_on, y), (other_on, y))

    @pl.when(jnp.logical_and(has_on, core == 0))
    def _():
        greet((other_on, y_back))

    @pl.when(jnp.logical_and(has_on, core == 1))
    def _():
        greet((other_on, y_on))

    @pl.when(has_back)
    def _():
        greet((own_back, y))

    loads = [
        pltpu.make_async_copy(emb_ref.at[pl.ds(c * part, part)], x_in.at[pl.ds(c * part, part)], load_sem.at[c])
        for c in range(chunks)
    ]
    for load in loads:
        load.start()

    small[0].wait()
    cols = cols_ref[...]
    nibble = lax.broadcasted_iota(jnp.int32, (16, kept), 0)
    low = parity_sign(nibble & (cols & 15)).astype(F32)
    high = parity_sign(nibble & ((cols >> 4) & 15)).astype(F32)
    for u in range(16):
        picked[pl.ds(u * 16, 16), :] = low * high[u:u + 1, :]

    def fill(run, carry):
        chosen = jnp.where((cols >> 8) == run, 1.0, 0.0)
        table[pl.ds(pl.multiple_of(run * HB, HB), HB), :] = (picked[pl.ds(0, HB), :] * chosen).astype(BF16)
        return carry

    lax.fori_loop(0, width // HB, fill, 0)

    small[1].wait()
    n_clusters = sizes_ref.shape[1]
    at = lax.broadcasted_iota(jnp.int32, (n_clusters, n_clusters), 0)
    upto = lax.broadcasted_iota(jnp.int32, (n_clusters, n_clusters), 1)
    ends = jnp.sum(jnp.where(upto <= at, sizes_ref[...], 0), axis=1, keepdims=True)

    def number(column, of_core, place):
        return (2 * column + of_core) * groups + place

    numbers = [
        number(t, core, y), number(t, core, y_back), number(t, core, y_two), number(t_back, core, y),
        number(t, 1 - core, y), number(t_on, 1 - core, y), number(wrap(t + core, columns), 1 - core, y_on),
        number(wrap(t - 1, columns), 1, groups - 1),
    ]
    for slot, block in enumerate(numbers):
        which = block * rows + lax.broadcasted_iota(jnp.int32, (n_clusters, rows), 1)
        ids = jnp.sum(jnp.where(ends <= which, 1.0, 0.0), axis=0, keepdims=True)
        lane_id[pl.ds(slot * 8, 8), :] = jnp.broadcast_to(ids, (8, rows))
        if slot in (A0, A1, A2, B0):
            row_id[pl.ds(slot * rows, rows), :] = jnp.broadcast_to(ids, (128, rows)).T
    row_best[...] = jnp.full_like(row_best, -1.0)
    lane_best[...] = jnp.full_like(lane_best, -1.0)

    def copy(source, target, c, device):
        return pltpu.make_async_remote_copy(
            src_ref=held.at[pl.ds(source * rows + c * part, part)],
            dst_ref=held.at[pl.ds(target * rows + c * part, part)],
            send_sem=send_sem.at[target, c],
            recv_sem=recv_sem.at[target, c],
            device_id=device,
            device_id_type=MESH,
        )

    def tile(left, left_at, count, right, right_at, lanes, own):
        rows_at = left * rows + left_at
        if not isinstance(rows_at, int):
            rows_at = pl.multiple_of(rows_at, 128)
        other_at = right * rows + right_at
        if not isinstance(other_at, int):
            other_at = pl.multiple_of(other_at, 128)
        scores = lax.dot_general(
            held[pl.ds(rows_at, count), :], held[pl.ds(other_at, lanes), :], (((1,), (1,)), ((), ())),
            preferred_element_type=F32,
        )
        left_ids = row_id[pl.ds(rows_at, count), :]
        best = row_best[pl.ds(rows_at, count), :]
        lane_row = right * 8 if isinstance(right, int) else pl.multiple_of(right * 8, 8)
        for j in range(lanes // 128):
            span = pl.ds(right_at + j * 128, 128)
            paired = left_ids == lane_id[pl.ds(lane_row, 8), span][0:1, :]
            if own:
                mine = left_at + lax.broadcasted_iota(jnp.int32, (count, 128), 0)
                theirs = right_at + j * 128 + lax.broadcasted_iota(jnp.int32, (count, 128), 1)
                paired = paired & (mine != theirs)
            masked = jnp.where(paired, scores[:, j * 128:(j + 1) * 128], -1.0)
            best = jnp.maximum(best, masked)
            if not own:
                lane_best[pl.ds(lane_row, 8), span] = jnp.maximum(
                    lane_best[pl.ds(lane_row, 8), span], jnp.max(masked.reshape(count // 8, 8, 128), axis=0)
                )
        row_best[pl.ds(rows_at, count), :] = best

    def tiles(left, right, left_part=None, right_part=None, own=False):
        for lc in range(chunks) if left_part is None else (left_part,):
            for rc in range(chunks) if right_part is None else (right_part,):
                tile(left, lc * part, part, right, rc * part, part, own)

    def close(slot):
        turned = row_best[pl.ds(slot * rows, rows), :].T
        lane_best[pl.ds(slot * 8, 8), :] = jnp.maximum(
            lane_best[pl.ds(slot * 8, 8), :], jnp.max(turned.reshape(16, 8, rows), axis=0)
        )

    def give(slot, device):
        return pltpu.make_async_remote_copy(
            src_ref=lane_best.at[pl.ds(slot * 8, 8)],
            dst_ref=landed.at[pl.ds(slot * 8, 8)],
            send_sem=back_send.at[slot],
            recv_sem=back_recv.at[slot],
            device_id=device,
            device_id_type=MESH,
        )

    sends_w = jnp.logical_and(jnp.logical_and(core == 1, y == 0), has_on)
    takes_w = jnp.logical_and(jnp.logical_and(core == 0, y == 0), has_on)
    x_out = [copy(A0, X0, c, (own_on, y)) for c in range(chunks)]
    y_out = [copy(X0, Y0, c, (other, y)) for c in range(chunks)]
    z_core0 = [copy(A1, Z, c, (other_on, y)) for c in range(chunks)]
    z_core1 = [copy(A1, Z, c, (other, y)) for c in range(chunks)]
    w_out = [copy(A1, W, c, (other_on, y)) for c in range(chunks)]
    back = {
        A1: give(A1, (blk, y_back)), A2: give(A2, (blk, y_two)), X0: give(X0, (own_back, y)), B0: give(B0, (other, y)),
        Y0: give(Y0, (other_on, y)), Z: give(Z, (z_to, y_on)),
        W: give(W, (2 * wrap(t - 1, columns) + 1, groups - 1)),
    }

    small[2].wait()
    signs = (2 * sign_ref[...] - 1).astype(F32).astype(BF16)
    sent = []
    for c in range(chunks):
        loads[c].wait()
        here = pl.ds(c * part, part)
        x_in[here, :] = x_in[here, :] * signs

        def project(n, total):
            span = pl.ds(pl.multiple_of(n * 256, 256), 256)
            some = jnp.dot(x_in[here, :], table[:, span], preferred_element_type=F32)
            picked[:, span] = some
            return total + some[:, :128] * some[:, :128] + some[:, 128:] * some[:, 128:]

        total = lax.fori_loop(0, kept // 256, project, jnp.zeros((part, 128), F32))
        scale = lax.rsqrt(jnp.sum(total, axis=1, keepdims=True) + 1e-6)
        held[here, :] = (picked[...] * scale).astype(BF16)
        if c == 0:
            pl.semaphore_wait(barrier, 5 + jnp.where(has_on, 3, 0) + jnp.where(has_back, 1, 0))

        for target, device in ((A1, (blk, y_on)), (B0, (other, y))):
            out = copy(A0, target, c, device)
            out.start()
            sent.append(out)

        @pl.when(has_on)
        def _():
            x_out[c].start()

    tiles(A0, A0, own=True)
    for c in range(chunks):
        copy(A0, B0, c, (other, y)).wait_recv()

    @pl.when(core == 1)
    def _():
        tiles(A0, B0)

    for c in range(chunks):
        copy(A0, A1, c, (blk, y_on)).wait_recv()
        out = copy(A1, A2, c, (blk, y_on))
        out.start()
        sent.append(out)

        @pl.when(jnp.logical_and(core == 0, has_on))
        def _():
            z_core0[c].start()

        @pl.when(core == 1)
        def _():
            z_core1[c].start()

        @pl.when(sends_w)
        def _():
            w_out[c].start()

        @pl.when(has_back)
        def _():
            x_out[c].wait_recv()
            y_out[c].start()
            tiles(A0, X0, right_part=c)

        tiles(A1, A0, left_part=c)

    @pl.when(has_back)
    def _():
        tiles(A1, X0)

    @pl.when(has_on)
    def _():
        for c in range(chunks):
            y_out[c].wait_recv()

    @pl.when(core == 0)
    def _():
        tiles(A1, B0)

    @pl.when(jnp.logical_and(core == 0, has_on))
    def _():
        tiles(A0, Y0)

    @pl.when(jnp.logical_and(core == 1, has_on))
    def _():
        tiles(A1, Y0)

    @pl.when(takes_w)
    def _():
        for c in range(chunks):
            w_out[c].wait_recv()
        tiles(B0, W)
        close(B0)

    close(A0)
    close(A1)
    back[A1].start()
    for c in range(chunks):
        copy(A1, A2, c, (blk, y_on)).wait_recv()
        tiles(A2, A0, left_part=c)

        @pl.when(has_back)
        def _():
            tiles(A2, X0, left_part=c)

        @pl.when(jnp.logical_and(core == 0, has_on))
        def _():
            tiles(A2, Y0, left_part=c)

        @pl.when(core == 1)
        def _():
            tiles(A2, B0, left_part=c)

        @pl.when(has_z)
        def _():
            z_core1[c].wait_recv()
            tiles(A2, Z, left_part=c, right_part=c)
            for before in range(c):
                tiles(A2, Z, left_part=c, right_part=before)
                tiles(A2, Z, left_part=before, right_part=c)

    @pl.when(jnp.logical_and(jnp.logical_and(core == 1, has_z), y == groups - 1))
    def _():
        tiles(B0, Z)
        close(B0)

    close(A2)
    back[A2].start()
    back[B0].start()

    @pl.when(has_back)
    def _():
        back[X0].start()

    @pl.when(has_on)
    def _():
        back[Y0].start()

    @pl.when(has_z)
    def _():
        back[Z].start()

    @pl.when(takes_w)
    def _():
        back[W].start()

    best = lane_best[pl.ds(A0 * 8, 8), :]
    for slot in (A1, A2, B0):
        back[slot].wait_recv()
        best = jnp.maximum(best, landed[pl.ds(slot * 8, 8), :])
    lane_best[pl.ds(A0 * 8, 8), :] = best

    def take(condition, slot):
        @pl.when(condition)
        def _():
            back[slot].wait_recv()
            lane_best[pl.ds(A0 * 8, 8), :] = jnp.maximum(
                lane_best[pl.ds(A0 * 8, 8), :], landed[pl.ds(slot * 8, 8), :]
            )

    take(has_on, X0)
    take(has_on, Y0)
    take(jnp.logical_or(core == 1, t > 0), Z)
    take(jnp.logical_and(jnp.logical_and(core == 1, has_on), y == groups - 1), W)
    out_ref[...] = jnp.max(lane_best[pl.ds(A0 * 8, 8), :], axis=0, keepdims=True)

    for out in (*sent, back[A1], back[A2], back[B0]):
        out.wait_send()
    for condition, outs in (
        (has_on, x_out), (has_back, y_out), (jnp.logical_and(core == 0, has_on), z_core0), (core == 1, z_core1),
        (sends_w, w_out), (has_back, [back[X0]]), (has_on, [back[Y0]]), (has_z, [back[Z]]), (takes_w, [back[W]]),
    ):
        @pl.when(condition)
        def _():
            for out in outs:
                out.wait_send()


def solution(mesh):
    blocks, groups = mesh.shape["blk"], mesh.shape["grp"]
    chunks = 2

    def local(embeddings, cluster_sizes, sign_bits, sample_cols):
        rows, width = embeddings.shape
        kept = sample_cols.shape[0]
        vmem = pl.BlockSpec(memory_space=pltpu.VMEM)
        hbm = pl.BlockSpec(memory_space=pltpu.HBM)
        best = pl.pallas_call(
            functools.partial(kernel, blocks, groups, chunks),
            out_shape=jax.ShapeDtypeStruct((1, rows), F32),
            in_specs=[hbm] * 4,
            out_specs=vmem,
            scratch_shapes=[
                pltpu.VMEM((1, cluster_sizes.shape[0]), jnp.int32),
                pltpu.VMEM((1, width), jnp.int32),
                pltpu.VMEM((1, kept), jnp.int32),
                pltpu.VMEM((8 * rows, kept), BF16),
                pltpu.VMEM((rows, width), BF16),
                pltpu.VMEM((width, kept), BF16),
                pltpu.VMEM((rows // chunks, kept), F32),
                pltpu.VMEM((5 * rows, 128), F32),
                pltpu.VMEM((64, rows), F32),
                pltpu.VMEM((5 * rows, 128), F32),
                pltpu.VMEM((64, rows), F32),
                pltpu.VMEM((64, rows), F32),
                pltpu.SemaphoreType.DMA((chunks,)),
                pltpu.SemaphoreType.DMA((3,)),
                pltpu.SemaphoreType.DMA((KINDS, chunks)),
                pltpu.SemaphoreType.DMA((KINDS, chunks)),
                pltpu.SemaphoreType.DMA((KINDS,)),
                pltpu.SemaphoreType.DMA((KINDS,)),
            ],
            compiler_params=pltpu.CompilerParams(
                collective_id=0, has_side_effects=True, vmem_limit_bytes=60 * 1024 * 1024
            ),
        )(embeddings, cluster_sizes.reshape(1, -1), sign_bits.reshape(1, -1), sample_cols.reshape(1, -1))
        return best.reshape(rows)

    placed = (P(("blk", "grp"), None), P(), P(), P())
    return jax.shard_map(local, mesh=mesh, in_specs=placed, out_specs=P(("blk", "grp")), check_vma=False)
```

time: 48.2 us -> 43.5 us (0.902)
  the two profiles are of different devices: /device:TPU:8 before, /device:TPU:103 now
where the time goes in v2:
time: 43.5 us; the launch traced here: 43.4 us
  Pallas kernels  42.1 us (97%)
  local copies, waits for them, and re-layouts  1.26 us (3%)
    pallas_call x1, Pallas kernels, local(): pl.pallas_call(functools.partial(kernel, blocks, groups, chunks), out_sha...  42.1 us
    unnamed x1, local copies, waits for them, and re-layouts  1.26 us

profile of v2, /device:TPU:103, one launch (start us, length us, event | category | flops | bytes accessed | tf_op | source)
XLA Modules:
  0.0 43.4 jit_solution(3196068638314191154)
XLA Ops:
  0.0 42.1 %shard_map.46 = f32[1,512]{1,0:T(1,128)} custom-call(bf16[512,4096]{1,0:T(8,128)(2,1)} %emb_ref.1, s32[1,128]{1,0:T(1,128)} %bitcast.7, s32[1,4096]{1,0:T(1,128)} %bitcast.4, s32[1,1024]{1,0:T(1,128)} %bitcast.6), custom_call_target="tpu_custom_call" | custom-call | tf_op jit(solution)/shard_map/pallas_call | solution.py:392
  42.1 1.3 %copy.6 = f32[512]{0:T(512)} copy(f32[512]{0:T(512)} %bitcast.5) | data formatting | bytes 4096

commit v3 on v2

--- a/solution.py
+++ b/solution.py
@@ -23,10 +23,13 @@
 
 
 def kernel(blocks, groups, chunks, emb_ref, sizes_in, sign_in, cols_in, out_ref, sizes_ref, sign_ref, cols_ref, held, x_in,
-           table, picked, row_best, lane_best, row_id, lane_id, landed, load_sem, small_sem, send_sem, recv_sem, back_send,
-           back_recv):
+           *rest):
+    tables = rest[:-12]
+    (picked, row_best, lane_best, row_id, lane_id, landed, load_sem, small_sem, send_sem, recv_sem, back_send,
+     back_recv) = rest[-12:]
     rows, width = x_in.shape
-    kept = table.shape[1]
+    lanes = tables[0].shape[1]
+    kept = lanes * len(tables)
     part = rows // chunks
     columns = blocks // 2
     blk = lax.axis_index("blk")
@@ -94,43 +97,36 @@
     for load in loads:
         load.start()
 
-    small[0].wait()
-    cols = cols_ref[...]
-    nibble = lax.broadcasted_iota(jnp.int32, (16, kept), 0)
-    low = parity_sign(nibble & (cols & 15)).astype(F32)
-    high = parity_sign(nibble & ((cols >> 4) & 15)).astype(F32)
-    for u in range(16):
-        picked[pl.ds(u * 16, 16), :] = low * high[u:u + 1, :]
-
-    def fill(run, carry):
-        chosen = jnp.where((cols >> 8) == run, 1.0, 0.0)
-        table[pl.ds(pl.multiple_of(run * HB, HB), HB), :] = (picked[pl.ds(0, HB), :] * chosen).astype(BF16)
-        return carry
-
-    lax.fori_loop(0, width // HB, fill, 0)
-
-    small[1].wait()
-    n_clusters = sizes_ref.shape[1]
-    at = lax.broadcasted_iota(jnp.int32, (n_clusters, n_clusters), 0)
-    upto = lax.broadcasted_iota(jnp.int32, (n_clusters, n_clusters), 1)
-    ends = jnp.sum(jnp.where(upto <= at, sizes_ref[...], 0), axis=1, keepdims=True)
+    def fill(n):
+        cols = cols_ref[:, n * lanes:(n + 1) * lanes]
+        nibble = lax.broadcasted_iota(jnp.int32, (16, lanes), 0)
+        low = parity_sign(nibble & (cols & 15))
+        high = parity_sign(nibble & ((cols >> 4) & 15))
+        table = jnp.concatenate([(low * high[u:u + 1, :]).astype(BF16) for u in range(16)], axis=0)
+        for run in range(width // HB):
+            chosen = jnp.broadcast_to(jnp.where((cols >> 8) == run, 1.0, 0.0), (16, lanes)).astype(BF16)
+            tables[n][pl.ds(run * HB, HB), :] = table * jnp.concatenate([chosen] * 16, axis=0)
 
     def number(column, of_core, place):
         return (2 * column + of_core) * groups + place
 
-    numbers = [
-        number(t, core, y), number(t, core, y_back), number(t, core, y_two), number(t_back, core, y),
-        number(t, 1 - core, y), number(t_on, 1 - core, y), number(wrap(t + core, columns), 1 - core, y_on),
-        number(wrap(t - 1, columns), 1, groups - 1),
-    ]
-    for slot, block in enumerate(numbers):
-        which = block * rows + lax.broadcasted_iota(jnp.int32, (n_clusters, rows), 1)
-        ids = jnp.sum(jnp.where(ends <= which, 1.0, 0.0), axis=0, keepdims=True)
-        lane_id[pl.ds(slot * 8, 8), :] = jnp.broadcast_to(ids, (8, rows))
-        if slot in (A0, A1, A2, B0):
-            row_id[pl.ds(slot * rows, rows), :] = jnp.broadcast_to(ids, (128, rows)).T
-    row_best[...] = jnp.full_like(row_best, -1.0)
-    lane_best[...] = jnp.full_like(lane_best, -1.0)
+    def name_clusters():
+        n_clusters = sizes_ref.shape[1]
+        at = lax.broadcasted_iota(jnp.int32, (n_clusters, n_clusters), 0)
+        upto = lax.broadcasted_iota(jnp.int32, (n_clusters, n_clusters), 1)
+        ends = jnp.sum(jnp.where(upto <= at, sizes_ref[...], 0), axis=1, keepdims=True)
+        numbers = [
+            number(t, core, y), number(t, core, y_back), number(t, core, y_two), number(t_back, core, y),
+            number(t, 1 - core, y), number(t_on, 1 - core, y), number(wrap(t + core, columns), 1 - core, y_on),
+            number(wrap(t - 1, columns), 1, groups - 1),
+        ]
+        for slot, block in enumerate(numbers):
+            which = block * rows + lax.broadcasted_iota(jnp.int32, (n_clusters, rows), 1)
+            ids = jnp.sum(jnp.where(ends <= which, 1.0, 0.0), axis=0, keepdims=True)
+            lane_id[pl.ds(slot * 8, 8), :] = jnp.broadcast_to(ids, (8, rows))
+            if slot in (A0, A1, A2, B0):
+                row_id[pl.ds(slot * rows, rows), :] = jnp.broadcast_to(ids, (128, rows)).T
+
 
     def copy(source, target, c, device):
         return pltpu.make_async_remote_copy(
@@ -171,15 +167,19 @@
                 )
         row_best[pl.ds(rows_at, count), :] = best
 
-    def tiles(left, right, left_part=None, right_part=None, own=False):
-        for lc in range(chunks) if left_part is None else (left_part,):
-            for rc in range(chunks) if right_part is None else (right_part,):
-                tile(left, lc * part, part, right, rc * part, part, own)
-
-    def close(slot):
-        turned = row_best[pl.ds(slot * rows, rows), :].T
-        lane_best[pl.ds(slot * 8, 8), :] = jnp.maximum(
-            lane_best[pl.ds(slot * 8, 8), :], jnp.max(turned.reshape(16, 8, rows), axis=0)
+    def tiles(left, right, left_parts=None, right_parts=None, own=False):
+        left_from, left_to = (0, chunks) if left_parts is None else left_parts
+        right_from, right_to = (0, chunks) if right_parts is None else right_parts
+        for lc in range(left_from, left_to, 2):
+            count = min(2, left_to - lc) * part
+            for rc in range(right_from, right_to, 2):
+                tile(left, lc * part, count, right, rc * part, min(2, right_to - rc) * part, own)
+
+    def close(slot, first=0, last=chunks):
+        span = pl.ds(first * part, (last - first) * part)
+        turned = row_best[pl.ds(slot * rows + first * part, (last - first) * part), :].T
+        lane_best[pl.ds(slot * 8, 8), span] = jnp.maximum(
+            lane_best[pl.ds(slot * 8, 8), span], jnp.max(turned.reshape(16, 8, (last - first) * part), axis=0)
         )
 
     def give(slot, device):
@@ -194,6 +194,8 @@
 
     sends_w = jnp.logical_and(jnp.logical_and(core == 1, y == 0), has_on)
     takes_w = jnp.logical_and(jnp.logical_and(core == 0, y == 0), has_on)
+    needs_far = jnp.logical_and(has_back, jnp.where(core == 1, y - groups // 2, groups // 2 - 1 - y) >= 0)
+    edge_z = jnp.logical_and(jnp.logical_and(core == 1, has_z), y == groups - 1)
     x_out = [copy(A0, X0, c, (own_on, y)) for c in range(chunks)]
     y_out = [copy(X0, Y0, c, (other, y)) for c in range(chunks)]
     z_core0 = [copy(A1, Z, c, (other_on, y)) for c in range(chunks)]
@@ -208,18 +210,19 @@
     small[2].wait()
     signs = (2 * sign_ref[...] - 1).astype(F32).astype(BF16)
     sent = []
+    small[0].wait()
     for c in range(chunks):
         loads[c].wait()
         here = pl.ds(c * part, part)
-        x_in[here, :] = x_in[here, :] * signs
-
-        def project(n, total):
-            span = pl.ds(pl.multiple_of(n * 256, 256), 256)
-            some = jnp.dot(x_in[here, :], table[:, span], preferred_element_type=F32)
-            picked[:, span] = some
-            return total + some[:, :128] * some[:, :128] + some[:, 128:] * some[:, 128:]
-
-        total = lax.fori_loop(0, kept // 256, project, jnp.zeros((part, 128), F32))
+        flipped = x_in[here, :] * signs
+        total = jnp.zeros((part, 128), F32)
+        for n in range(len(tables)):
+            if c == 0:
+                fill(n)
+            some = jnp.dot(flipped, tables[n][...], preferred_element_type=F32)
+            picked[:, n * lanes:(n + 1) * lanes] = some
+            for k in range(0, lanes, 128):
+                total = total + some[:, k:k + 128] * some[:, k:k + 128]
         scale = lax.rsqrt(jnp.sum(total, axis=1, keepdims=True) + 1e-6)
         held[here, :] = (picked[...] * scale).astype(BF16)
         if c == 0:
@@ -234,6 +237,10 @@
         def _():
             x_out[c].start()
 
+    row_best[...] = jnp.full_like(row_best, -1.0)
+    lane_best[...] = jnp.full_like(lane_best, -1.0)
+    small[1].wait()
+    name_clusters()
     tiles(A0, A0, own=True)
     for c in range(chunks):
         copy(A0, B0, c, (other, y)).wait_recv()
@@ -264,9 +271,13 @@
         def _():
             x_out[c].wait_recv()
             y_out[c].start()
-            tiles(A0, X0, right_part=c)
-
-        tiles(A1, A0, left_part=c)
+
+        if c % 2:
+            tiles(A1, A0, left_parts=(c - 1, c + 1))
+
+            @pl.when(has_back)
+            def _():
+                tiles(A0, X0, right_parts=(c - 1, c + 1))
 
     @pl.when(has_back)
     def _():
@@ -289,71 +300,90 @@
     def _():
         tiles(A1, Y0)
 
-    @pl.when(takes_w)
-    def _():
-        for c in range(chunks):
-            w_out[c].wait_recv()
-        tiles(B0, W)
-        close(B0)
-
-    close(A0)
     close(A1)
     back[A1].start()
+
+    @pl.when(jnp.logical_and(core == 0, jnp.logical_not(takes_w)))
+    def _():
+        back[B0].start()
+
+    @pl.when(jnp.logical_and(core == 1, has_on))
+    def _():
+        back[Y0].start()
+
     for c in range(chunks):
         copy(A1, A2, c, (blk, y_on)).wait_recv()
-        tiles(A2, A0, left_part=c)
-
-        @pl.when(has_back)
-        def _():
-            tiles(A2, X0, left_part=c)
+        one = (c, c + 1)
+
+        @pl.when(needs_far)
+        def _():
+            tiles(A2, X0, left_parts=one)
 
         @pl.when(jnp.logical_and(core == 0, has_on))
         def _():
-            tiles(A2, Y0, left_part=c)
+            tiles(A2, Y0, left_parts=one)
 
         @pl.when(core == 1)
         def _():
-            tiles(A2, B0, left_part=c)
-
-        @pl.when(has_z)
-        def _():
-            z_core1[c].wait_recv()
-            tiles(A2, Z, left_part=c, right_part=c)
-            for before in range(c):
-                tiles(A2, Z, left_part=c, right_part=before)
-                tiles(A2, Z, left_part=before, right_part=c)
-
-    @pl.when(jnp.logical_and(jnp.logical_and(core == 1, has_z), y == groups - 1))
-    def _():
-        tiles(B0, Z)
+            tiles(A2, B0, left_parts=one)
+
+        if c == chunks - 1:
+
+            @pl.when(has_back)
+            def _():
+                back[X0].start()
+
+            @pl.when(jnp.logical_and(core == 0, has_on))
+            def _():
+                back[Y0].start()
+
+            @pl.when(jnp.logical_and(core == 1, jnp.logical_not(edge_z)))
+            def _():
+                back[B0].start()
+
+        tiles(A2, A0, left_parts=one)
+        if c % 2:
+            two = (c - 1, c + 1)
+
+            @pl.when(has_z)
+            def _():
+                for k in range(*two):
+                    z_core1[k].wait_recv()
+                tiles(A2, Z, left_parts=(0, c + 1), right_parts=two)
+                if c > 1:
+                    tiles(A2, Z, left_parts=two, right_parts=(0, c - 1))
+
+            if c == chunks - 1:
+                close(A2)
+                back[A2].start()
+
+                @pl.when(jnp.logical_and(has_z, jnp.logical_not(edge_z)))
+                def _():
+                    back[Z].start()
+
+            @pl.when(edge_z)
+            def _():
+                tiles(B0, Z, right_parts=two)
+
+            @pl.when(takes_w)
+            def _():
+                for k in range(*two):
+                    w_out[k].wait_recv()
+                tiles(B0, W, right_parts=two)
+
+    @pl.when(edge_z)
+    def _():
+        back[Z].start()
         close(B0)
-
-    close(A2)
-    back[A2].start()
-    back[B0].start()
-
-    @pl.when(has_back)
-    def _():
-        back[X0].start()
-
-    @pl.when(has_on)
-    def _():
-        back[Y0].start()
-
-    @pl.when(has_z)
-    def _():
-        back[Z].start()
+        back[B0].start()
 
     @pl.when(takes_w)
     def _():
         back[W].start()
-
-    best = lane_best[pl.ds(A0 * 8, 8), :]
-    for slot in (A1, A2, B0):
-        back[slot].wait_recv()
-        best = jnp.maximum(best, landed[pl.ds(slot * 8, 8), :])
-    lane_best[pl.ds(A0 * 8, 8), :] = best
-
+        close(B0)
+        back[B0].start()
+
+    close(A0)
     def take(condition, slot):
         @pl.when(condition)
         def _():
@@ -364,6 +394,11 @@
 
     take(has_on, X0)
     take(has_on, Y0)
+    for slot in (A1, B0, A2):
+        back[slot].wait_recv()
+    lane_best[pl.ds(A0 * 8, 8), :] = functools.reduce(
+        jnp.maximum, [lane_best[pl.ds(A0 * 8, 8), :], *(landed[pl.ds(slot * 8, 8), :] for slot in (A1, B0, A2))]
+    )
     take(jnp.logical_or(core == 1, t > 0), Z)
     take(jnp.logical_and(jnp.logical_and(core == 1, has_on), y == groups - 1), W)
     out_ref[...] = jnp.max(lane_best[pl.ds(A0 * 8, 8), :], axis=0, keepdims=True)
@@ -382,7 +417,7 @@
 
 def solution(mesh):
     blocks, groups = mesh.shape["blk"], mesh.shape["grp"]
-    chunks = 2
+    chunks, lanes = 4, 256
 
     def local(embeddings, cluster_sizes, sign_bits, sample_cols):
         rows, width = embeddings.shape
@@ -400,7 +435,7 @@
                 pltpu.VMEM((1, kept), jnp.int32),
                 pltpu.VMEM((8 * rows, kept), BF16),
                 pltpu.VMEM((rows, width), BF16),
-                pltpu.VMEM((width, kept), BF16),
+                *[pltpu.VMEM((width, lanes), BF16) for _ in range(kept // lanes)],
                 pltpu.VMEM((rows // chunks, kept), F32),
                 pltpu.VMEM((5 * rows, 128), F32),
                 pltpu.VMEM((64, rows), F32),

time: 43.5 us -> 39.5 us (0.908)
  the two profiles are of different devices: /device:TPU:103 before, /device:TPU:128 now
where the time goes in v3:
time: 39.5 us; the launch traced here: 39.4 us
  Pallas kernels  38.1 us (96%)
  local copies, waits for them, and re-layouts  1.26 us (3%)
    pallas_call x1, Pallas kernels, local(): pl.pallas_call(functools.partial(kernel, blocks, groups, chunks), out_sha...  38.1 us
    unnamed x1, local copies, waits for them, and re-layouts  1.26 us

profile of v3, /device:TPU:128, one launch (start us, length us, event | category | flops | bytes accessed | tf_op | source)
XLA Modules:
  0.0 39.4 jit_solution(9467132297564189041)
XLA Ops:
  0.0 38.1 %shard_map.46 = f32[1,512]{1,0:T(1,128)} custom-call(bf16[512,4096]{1,0:T(8,128)(2,1)} %emb_ref.1, s32[1,128]{1,0:T(1,128)} %bitcast.7, s32[1,4096]{1,0:T(1,128)} %bitcast.4, s32[1,1024]{1,0:T(1,128)} %bitcast.6), custom_call_target="tpu_custom_call" | custom-call | tf_op jit(solution)/shard_map/pallas_call | solution.py:427
  38.1 1.3 %copy.6 = f32[512]{0:T(512)} copy(f32[512]{0:T(512)} %bitcast.5) | data formatting | bytes 4096

commit v4 on v3

--- a/solution.py
+++ b/solution.py
@@ -31,6 +31,7 @@
     lanes = tables[0].shape[1]
     kept = lanes * len(tables)
     part = rows // chunks
+    joint = 256 // part
     columns = blocks // 2
     blk = lax.axis_index("blk")
     y = lax.axis_index("grp")
@@ -64,27 +65,11 @@
     for load in small:
         load.start()
 
-    greet((blk, y_on), (blk, y_back), (blk, y_two), (other, y))
-
-    @pl.when(core == 0)
-    def _():
-        greet((other, y_on))
-
-    @pl.when(core == 1)
-    def _():
-        greet((other, y_back))
+    greet((blk, y_on), (blk, y_back), (other, y))
 
     @pl.when(has_on)
     def _():
         greet((own_on, y), (other_on, y))
-
-    @pl.when(jnp.logical_and(has_on, core == 0))
-    def _():
-        greet((other_on, y_back))
-
-    @pl.when(jnp.logical_and(has_on, core == 1))
-    def _():
-        greet((other_on, y_on))
 
     @pl.when(has_back)
     def _():
@@ -170,10 +155,10 @@
     def tiles(left, right, left_parts=None, right_parts=None, own=False):
         left_from, left_to = (0, chunks) if left_parts is None else left_parts
         right_from, right_to = (0, chunks) if right_parts is None else right_parts
-        for lc in range(left_from, left_to, 2):
-            count = min(2, left_to - lc) * part
-            for rc in range(right_from, right_to, 2):
-                tile(left, lc * part, count, right, rc * part, min(2, right_to - rc) * part, own)
+        for lc in range(left_from, left_to, joint):
+            count = min(joint, left_to - lc) * part
+            for rc in range(right_from, right_to, joint):
+                tile(left, lc * part, count, right, rc * part, min(joint, right_to - rc) * part, own)
 
     def close(slot, first=0, last=chunks):
         span = pl.ds(first * part, (last - first) * part)
@@ -194,7 +179,8 @@
 
     sends_w = jnp.logical_and(jnp.logical_and(core == 1, y == 0), has_on)
     takes_w = jnp.logical_and(jnp.logical_and(core == 0, y == 0), has_on)
-    needs_far = jnp.logical_and(has_back, jnp.where(core == 1, y - groups // 2, groups // 2 - 1 - y) >= 0)
+    far = jnp.where(core == 1, y - groups // 2, groups // 2 - 1 - y) >= 0
+    needs_far = jnp.logical_and(has_back, far)
     edge_z = jnp.logical_and(jnp.logical_and(core == 1, has_z), y == groups - 1)
     x_out = [copy(A0, X0, c, (own_on, y)) for c in range(chunks)]
     y_out = [copy(X0, Y0, c, (other, y)) for c in range(chunks)]
@@ -226,16 +212,16 @@
         scale = lax.rsqrt(jnp.sum(total, axis=1, keepdims=True) + 1e-6)
         held[here, :] = (picked[...] * scale).astype(BF16)
         if c == 0:
-            pl.semaphore_wait(barrier, 5 + jnp.where(has_on, 3, 0) + jnp.where(has_back, 1, 0))
+            pl.semaphore_wait(barrier, 3 + jnp.where(has_on, 2, 0) + jnp.where(has_back, 1, 0))
+
+        @pl.when(has_on)
+        def _():
+            x_out[c].start()
 
         for target, device in ((A1, (blk, y_on)), (B0, (other, y))):
             out = copy(A0, target, c, device)
             out.start()
             sent.append(out)
-
-        @pl.when(has_on)
-        def _():
-            x_out[c].start()
 
     row_best[...] = jnp.full_like(row_best, -1.0)
     lane_best[...] = jnp.full_like(lane_best, -1.0)
@@ -272,12 +258,13 @@
             x_out[c].wait_recv()
             y_out[c].start()
 
-        if c % 2:
-            tiles(A1, A0, left_parts=(c - 1, c + 1))
+        if c % joint == joint - 1:
+            two = (c - joint + 1, c + 1)
+            tiles(A1, A0, left_parts=two)
 
             @pl.when(has_back)
             def _():
-                tiles(A0, X0, right_parts=(c - 1, c + 1))
+                tiles(A0, X0, right_parts=two)
 
     @pl.when(has_back)
     def _():
@@ -341,29 +328,36 @@
             def _():
                 back[B0].start()
 
-        tiles(A2, A0, left_parts=one)
-        if c % 2:
-            two = (c - 1, c + 1)
+        @pl.when(jnp.logical_not(far))
+        def _():
+            tiles(A2, A0, left_parts=one)
+
+        if c % joint == joint - 1:
+            two = (c - joint + 1, c + 1)
 
             @pl.when(has_z)
             def _():
                 for k in range(*two):
                     z_core1[k].wait_recv()
+
+            @pl.when(edge_z)
+            def _():
+                tiles(B0, Z, right_parts=two)
+
+            @pl.when(has_z)
+            def _():
                 tiles(A2, Z, left_parts=(0, c + 1), right_parts=two)
-                if c > 1:
-                    tiles(A2, Z, left_parts=two, right_parts=(0, c - 1))
+                if c >= joint:
+                    tiles(A2, Z, left_parts=two, right_parts=(0, c - joint + 1))
 
             if c == chunks - 1:
+
+                @pl.when(has_z)
+                def _():
+                    back[Z].start()
+
                 close(A2)
                 back[A2].start()
-
-                @pl.when(jnp.logical_and(has_z, jnp.logical_not(edge_z)))
-                def _():
-                    back[Z].start()
-
-            @pl.when(edge_z)
-            def _():
-                tiles(B0, Z, right_parts=two)
 
             @pl.when(takes_w)
             def _():
@@ -373,7 +367,6 @@
 
     @pl.when(edge_z)
     def _():
-        back[Z].start()
         close(B0)
         back[B0].start()
 

time: 39.5 us -> 39.3 us (level)
  no operation moved by 1% of the time
where the time goes in v4:
time: 39.3 us; the launch traced here: 39.2 us
  Pallas kernels  38 us (97%)
  local copies, waits for them, and re-layouts  1.26 us (3%)
    pallas_call x1, Pallas kernels, local(): pl.pallas_call(functools.partial(kernel, blocks, groups, chunks), out_sha...  38 us
    unnamed x1, local copies, waits for them, and re-layouts  1.26 us

profile of v4, /device:TPU:128, one launch (start us, length us, event | category | flops | bytes accessed | tf_op | source)
XLA Modules:
  0.0 39.2 jit_solution(18437224675272413694)
XLA Ops:
  0.0 38.0 %shard_map.46 = f32[1,512]{1,0:T(1,128)} custom-call(bf16[512,4096]{1,0:T(8,128)(2,1)} %emb_ref.1, s32[1,128]{1,0:T(1,128)} %bitcast.7, s32[1,4096]{1,0:T(1,128)} %bitcast.4, s32[1,1024]{1,0:T(1,128)} %bitcast.6), custom_call_target="tpu_custom_call" | custom-call | tf_op jit(solution)/shard_map/pallas_call | solution.py:420
  38.0 1.3 %copy.6 = f32[512]{0:T(512)} copy(f32[512]{0:T(512)} %bitcast.5) | data formatting | bytes 4096
